TPU v7x, 512 devices: a whole 4x4x16 slice. The times are simulated.
512 devices in a mesh: mesh: 32 (over z, core), run: 16 (over y, x).
Axes of the slice: x: 4, y: 4, z: 16, core: 2. Of those that a mesh axis runs over, the one named last changes fastest.
Arguments:
- snapshots: bfloat16 [65536, 2048], P('mesh', 'run'), may hold values from -6 to 6
- block_cols: int32 [1024, 16], P('mesh'), may hold values from 0 to 1023, as said below
- mass_blocks: bfloat16 [1024, 64, 1024], P('mesh'), as said below
Outputs:
- gram: float32 [2048, 2048], P('mesh', 'run')
Inputs may be any that keep to these rules, and one draw needn't show every extreme that they name: `block_cols`: block row b names 16 different block columns, the first of them b itself; all lie from 2 blocks before the first block row of shard b // 32 to 2 blocks after its last. In every shard but the first, its first block row names the block 2 before the shard; in every shard but the last, its last block row names the block 2 after it. `mass_blocks`: entry [b, i, k * 64 + j] is row i, column j of the k-th stored block of block row b, in the order of block_cols.
All inputs are finite; a program needn't handle non-finite values.
Results may differ from a plain program's by a relative error of at most 0.00056.
Values may be sent and summed in bfloat16 or wider, within the bound.
A program may use at most 64 MiB of HBM per device.

v0:
```python
import jax
import jax.numpy as jnp
from jax import lax
from jax.sharding import PartitionSpec as P

BLK = 64
HB = 2


def extended(block, sides, width):
    for axis, dim in sides:
        count = lax.axis_size(axis)
        forward = [(i, i + 1) for i in range(count - 1)]
        backward = [(target, source) for source, target in forward]
        low = lax.ppermute(
            lax.slice_in_dim(block, block.shape[dim] - width, None, axis=dim), axis, forward
        )
        high = lax.ppermute(lax.slice_in_dim(block, 0, width, axis=dim), axis, backward)
        block = jnp.concatenate([low, block, high], axis=dim)
    return block


def contract_nodes(left_cols, right_cols):
    return lax.dot_general(
        left_cols, right_cols, (((0,), (0,)), ((), ())), preferred_element_type=jnp.float32
    )


def on_device(snapshots, block_cols, mass_blocks):
    node_count = snapshots.shape[0]
    column_count = snapshots.shape[1]
    blocks_here = node_count // BLK
    stored_count = block_cols.shape[1]
    rim_width = HB * BLK
    padded = extended(snapshots, (("mesh", 0),), rim_width)
    shard_index = lax.axis_index("mesh")
    local_cols = block_cols - (shard_index * blocks_here - HB)
    blocked = padded.reshape(blocks_here + 2 * HB, BLK, column_count)
    picked = blocked[local_cols].reshape(blocks_here, stored_count * BLK, column_count)
    weighted = jnp.einsum("bim,bmc->bic", mass_blocks, picked, preferred_element_type=jnp.float32)
    weighted = weighted.astype(jnp.bfloat16).reshape(node_count, column_count)
    gathered = lax.all_gather(snapshots, "run", axis=1, tiled=True)
    partial_term = contract_nodes(gathered, weighted)
    gram = lax.psum_scatter(partial_term, "mesh", scatter_dimension=0, tiled=True)
    return gram


def solution(mesh):
    placed = (P("mesh", "run"), P("mesh", None), P("mesh", None, None))
    return jax.shard_map(
        on_device, mesh=mesh, in_specs=placed, out_specs=P("mesh", "run"), check_vma=False
    )
```

profile of v0, /device:TPU:2, one launch (start us, length us, event | category | flops | bytes accessed | tf_op | source)
XLA Modules:
  0.0 229.1 jit_solution(6387576160055392372)
XLA Ops:
  6.5 0.0 all-gather.2.cloned.1.call-start
  6.5 0.7 all-gather.2.cloned.1.call-update
  7.3 0.0 reduce-scatter.4.cloned.1.call-start
  7.3 0.8 fusion
  8.1 1.7 collective-permute-start
  9.8 1.3 collective-permute-start.1
  11.1 0.7 compare_select_fusion
  11.8 0.1 copy.7
  11.9 0.1 reshape.14
  12.0 0.0 collective-permute-done
  12.0 2.6 %collective-permute-done.1 = bf16[128,128]{1,0:T(8,128)(2,1)S(1)} collective-permute-done((bf16[128,128]{1,0:T(8,128)(2,1)S(1)}, bf16[128,128]{1,0:T(8,128)(2,1)S(1)}, u32[]{:S(2)}, u32[]{:S(2)}) %collective-permute-start.1) | collective-permute-done | bytes 32800 | tf_op jit(solution)/shard_map/ppermute | solution.py:18
  14.6 1.1 pad_maximum_fusion
  15.7 13.4 %gather_fusion = bf16[512,64,128]{2,1,0:T(8,128)(2,1)} fusion(bf16[36,64,128]{2,1,0:T(8,128)(2,1)S(1)} %bitcast.12, s32[1024]{0:T(1024)S(1)} %pad_clamp_fusion), kind=kCustom, calls=%fused_computation | custom fusion | bytes 16779264 | tf_op jit(solution)/shard_map/gather | solution.py:39
  29.1 6.6 %convolution_convert_fusion = bf16[32,128,64]{1,2,0:T(8,128)(2,1)S(1)} fusion(bf16[32,64,1024]{2,1,0:T(8,128)(2,1)} %param.5, bf16[32,1024,128]{2,1,0:T(8,128)(2,1)} %bitcast.13), kind=kOutput, calls=%fused_computation.2 | convolution fusion | flops 537133056 | bytes 13107200 | tf_op jit(solution)/shard_map/bim,bmc->bic/dot_general | solution.py:40
  35.8 72.4 %all-gather.2.cloned.1.call-done = bf16[2048,2048]{1,0:T(8,128)(2,1)} async-done(((bf16[2048,128]{1,0:T(8,128)(2,1)}), bf16[2048,2048]{1,0:T(8,128)(2,1)}) %all-gather.2.cloned.1.call-update) | async-done | bytes 8388624 | tf_op jit(solution)/shard_map/all_gather | solution.py:42
  108.2 4.7 %convolution_bitcast_fusion = f32[2048,128]{0,1:T(8,128)S(1)} fusion(bf16[2048,128]{1,0:T(8,128)(2,1)S(1)} %bitcast.14, bf16[2048,2048]{1,0:T(8,128)(2,1)} %all-gather.2.cloned.1.call-done), kind=kOutput, calls=%fused_computation.1 | convolution fusion | flops 1073741824 | bytes 9961472 | tf_op jit(solution)/shard_map/dot_general | solution.py:24
  112.9 1.3 copy.9
  114.2 0.0 reduce-scatter.4.cloned.1.call-update
  114.2 108.1 %reduce-scatter.4.cloned.1.call-done = f32[64,128]{1,0:T(8,128)} async-done(((f32[2048,128]{1,0:T(8,128)}), f32[64,128]{1,0:T(8,128)}) %reduce-scatter.4.cloned.1.call-update) | async-done | bytes 32784 | tf_op jit(solution)/shard_map/reduce_scatter | solution.py:44
  (1 shorter events, 0.0 us)
Async XLA Ops:
  6.5 101.7 %all-gather.2.cloned.1.call-start = ((), (), s32[]{:S(2)}) async-start(), calls=%async_computation.1 | async-start | bytes 8912896 | tf_op jit(solution)/shard_map/all_gather | solution.py:42
  7.3 215.0 %reduce-scatter.4.cloned.1.call-start = ((), (), s32[]{:S(2)}) async-start(), calls=%async_computation.2 | async-start | bytes 1081344 | tf_op jit(solution)/shard_map/reduce_scatter | solution.py:44
  8.1 3.9 %collective-permute-start = (bf16[128,128]{1,0:T(8,128)(2,1)S(1)}, bf16[128,128]{1,0:T(8,128)(2,1)S(1)}, u32[]{:S(2)}, u32[]{:S(2)}) collective-permute-start(bf16[128,128]{1,0:T(8,128)(2,1)S(1)} %get-tuple-element.5), channel_id=1, source_target_pairs={{0,16},{16,32},{32,48},{48,64},{64,80},{80,96},{96,112},{112,128},... | collective-permute-start | bytes 98312 | tf_op jit(solution)/shard_map/ppermute | solution.py:15
  9.8 4.8 %collective-permute-start.1 = (bf16[128,128]{1,0:T(8,128)(2,1)S(1)}, bf16[128,128]{1,0:T(8,128)(2,1)S(1)}, u32[]{:S(2)}, u32[]{:S(2)}) collective-permute-start(bf16[128,128]{1,0:T(8,128)(2,1)S(1)} %get-tuple-element.6), channel_id=1, source_target_pairs={{16,0},{32,16},{48,32},{64,48},{80,64},{96,80},{112,96},{128,112},... | collective-permute-start | bytes 98312 | tf_op jit(solution)/shard_map/ppermute | solution.py:18
Sparse Core Ops, SparseCore 0:
  10.3 97.8 all-gather.1
  114.3 107.9 reduce-scatter.3
where the time goes:
time: 229 us
  waiting for transfers between devices  184 us (80%)
  local copies, waits for them, and re-layouts  15.7 us (7%)
  between operations  13.4 us (6%)
  matrix products  11.3 us (5%)
  starting transfers between devices  3.06 us (1%)
    reduce_scatter x1, waiting for transfers between devices, on_device(): lax.psum_scatter(partial_term, 'mesh', scatter_dimension=0, tiled=True)  108 us
    all_gather x1, waiting for transfers between devices, on_device(): gathered = lax.all_gather(snapshots, 'run', axis=1, tiled=True)  72.4 us
    gather x1, local copies, waits for them, and re-layouts, on_device(): blocked[local_cols].reshape(blocks_here, stored_count * BLK, column_count)  13.4 us
    dot_general x1, matrix products, on_device(): jnp.einsum('bim,bmc->bic', mass_blocks, picked, preferred_element_type=jn...  6.61 us
    dot_general x1, matrix products, contract_nodes(): lax.dot_general(left_cols, right_cols, (((0,), (0,)), ((), ())), preferre...  4.66 us
  transfers between devices with their start and end apart: 4, of which 3 were waited for; matrix products, arithmetic and copies ran while one was open for 10% of the time, Pallas kernels for 0%

commit v1 on v0

--- a/solution.py
+++ b/solution.py
@@ -5,6 +5,11 @@
 
 BLK = 64
 HB = 2
+
+
+def all_by_exchange(x, axis, along):
+    outgoing = jnp.stack([x] * lax.axis_size(axis))
+    return jnp.concatenate(lax.all_to_all(outgoing, axis, 0, 0), axis=along)
 
 
 def extended(block, sides, width):
@@ -39,7 +44,7 @@
     picked = blocked[local_cols].reshape(blocks_here, stored_count * BLK, column_count)
     weighted = jnp.einsum("bim,bmc->bic", mass_blocks, picked, preferred_element_type=jnp.float32)
     weighted = weighted.astype(jnp.bfloat16).reshape(node_count, column_count)
-    gathered = lax.all_gather(snapshots, "run", axis=1, tiled=True)
+    gathered = all_by_exchange(snapshots, "run", 1)
     partial_term = contract_nodes(gathered, weighted)
     gram = lax.psum_scatter(partial_term, "mesh", scatter_dimension=0, tiled=True)
     return gram

time: 229 us -> 269 us (1.17)
  waiting for transfers between devices: 184 us -> 210 us
  starting transfers between devices: 3.06 us -> 13.1 us
  local copies, waits for them, and re-layouts: 15.7 us -> 20.5 us
    all_to_all x0 -> x1, waiting for transfers between devices: none -> 90.6 us  [all_by_exchange(): return jnp.concatenate(lax.all_to_all(outgoing, axis, 0, 0), axis=along)]
    all_gather x1 -> x0, waiting for transfers between devices: 72.4 us -> none  [on_device(): gathered = lax.all_gather(snapshots, 'run', axis=1, tiled=True)]
    all_to_all x0 -> x1, starting transfers between devices: none -> 10.5 us  [all_by_exchange(): return jnp.concatenate(lax.all_to_all(outgoing, axis, 0, 0), axis=along)]
    reduce_scatter x1, waiting for transfers between devices: 108 us -> 117 us  [on_device(): lax.psum_scatter(partial_term, 'mesh', scatter_dimension=0, tiled=True)]
    another operation x0 -> x1, local copies, waits for them, and re-layouts: none -> 4.32 us  [all_by_exchange(): outgoing = jnp.stack([x] * lax.axis_size(axis))]
  transfers between devices with their start and end apart: 4 -> 4, of which waited for: 3 -> 3; matrix products, arithmetic and copies ran while one was open for 10% -> 7% of each run, Pallas kernels for 0% -> 0%
where the time goes in v1:
time: 269 us
  waiting for transfers between devices  210 us (78%)
  local copies, waits for them, and re-layouts  20.5 us (8%)
  between operations  13.5 us (5%)
  starting transfers between devices  13.1 us (5%)
  matrix products  12.5 us (5%)
    reduce_scatter x1, waiting for transfers between devices, on_device(): lax.psum_scatter(partial_term, 'mesh', scatter_dimension=0, tiled=True)  117 us
    all_to_all x1, waiting for transfers between devices, all_by_exchange(): return jnp.concatenate(lax.all_to_all(outgoing, axis, 0, 0), axis=along)  90.6 us
    gather x1, local copies, waits for them, and re-layouts, on_device(): blocked[local_cols].reshape(blocks_here, stored_count * BLK, column_count)  13.5 us
    all_to_all x1, starting transfers between devices, all_by_exchange(): return jnp.concatenate(lax.all_to_all(outgoing, axis, 0, 0), axis=along)  10.5 us
    dot_general x1, matrix products, contract_nodes(): lax.dot_general(left_cols, right_cols, (((0,), (0,)), ((), ())), preferre...  6.29 us
    dot_general x1, matrix products, on_device(): jnp.einsum('bim,bmc->bic', mass_blocks, picked, preferred_element_type=jn...  6.21 us
  transfers between devices with their start and end apart: 4, of which 3 were waited for; matrix products, arithmetic and copies ran while one was open for 7% of the time, Pallas kernels for 0%

profile of v1, /device:TPU:2, one launch (start us, length us, event | category | flops | bytes accessed | tf_op | source)
XLA Modules:
  0.0 269.2 jit_solution(7395607582551731409)
XLA Ops:
  6.5 1.2 copy.9
  7.8 4.3 %stack.2 = bf16[16,2048,128]{1,2,0:T(8,128)(2,1)} broadcast(bf16[2048,128]{0,1:T(8,128)(2,1)S(1)} %copy.9), dimensions={1,2} | broadcast | bytes 8912896 | tf_op jit(solution)/shard_map/stack | solution.py:11
  12.1 0.0 copy-start
  12.1 0.0 copy-start.1
  12.1 10.5 %all-to-all-start = ((bf16[16,2048,128]{1,2,0:T(8,128)(2,1)}), bf16[16,2048,128]{1,2,0:T(8,128)(2,1)}, u32[]{:S(2)}, u32[]{:S(2)}) async-start(bf16[16,2048,128]{1,2,0:T(8,128)(2,1)} %stack.2), calls=%async_computation | async-start | bytes 16777216 | tf_op jit(solution)/shard_map/all_to_all | solution.py:12
  22.6 0.0 reduce-scatter.4.cloned.1.call-start
  22.7 0.0 copy-done
  22.7 1.3 collective-permute-start
  24.0 1.3 collective-permute-start.1
  25.3 0.0 copy-done.1
  25.3 0.1 copy.8
  25.4 0.1 reshape.24
  25.5 0.0 collective-permute-done
  25.5 1.6 collective-permute-done.1
  27.1 13.5 %gather_fusion = bf16[512,64,128]{2,1,0:T(8,128)(2,1)} fusion(bf16[36,64,128]{2,1,0:T(8,128)(2,1)S(1)} %bitcast.15, s32[1024]{0:T(1024)S(1)} %pad_clamp_fusion), kind=kCustom, calls=%fused_computation | custom fusion | bytes 16779264 | tf_op jit(solution)/shard_map/gather | solution.py:44
  40.6 6.2 %convolution_convert_fusion = bf16[32,128,64]{1,2,0:T(8,128)(2,1)S(1)} fusion(bf16[32,64,1024]{2,1,0:T(8,128)(2,1)} %param.5, bf16[32,1024,128]{2,1,0:T(8,128)(2,1)} %bitcast.16), kind=kOutput, calls=%fused_computation.2 | convolution fusion | flops 537133056 | bytes 13107200 | tf_op jit(solution)/shard_map/bim,bmc->bic/dot_general | solution.py:45
  46.8 90.6 %all-to-all-done = bf16[16,2048,128]{1,2,0:T(8,128)(2,1)} async-done(((bf16[16,2048,128]{1,2,0:T(8,128)(2,1)}), bf16[16,2048,128]{1,2,0:T(8,128)(2,1)}, u32[]{:S(2)}, u32[]{:S(2)}) %all-to-all-start) | async-done | bytes 8388640 | tf_op jit(solution)/shard_map/all_to_all | solution.py:12
  137.5 6.3 %convolution_bitcast_fusion = f32[2048,128]{0,1:T(8,128)S(1)} fusion(bf16[2048,128]{1,0:T(8,128)(2,1)S(1)} %bitcast.17, bf16[2048,2048]{0,1:T(8,128)(2,1)} %bitcast.5), kind=kOutput, calls=%fused_computation.1 | convolution fusion | flops 1073741824 | bytes 9961472 | tf_op jit(solution)/shard_map/dot_general | solution.py:29
  143.8 1.3 copy.11
  145.1 0.0 reduce-scatter.4.cloned.1.call-update
  145.1 117.3 %reduce-scatter.4.cloned.1.call-done = f32[64,128]{1,0:T(8,128)} async-done(((f32[2048,128]{1,0:T(8,128)}), f32[64,128]{1,0:T(8,128)}) %reduce-scatter.4.cloned.1.call-update) | async-done | bytes 32784 | tf_op jit(solution)/shard_map/reduce_scatter | solution.py:49
  (4 shorter events, 0.1 us)
Async XLA Ops:
  12.1 10.6 %copy-start = (bf16[2048,128]{1,0:T(8,128)(2,1)S(1)}, bf16[2048,128]{1,0:T(8,128)(2,1)}, u32[]{:S(2)}) copy-start(bf16[2048,128]{1,0:T(8,128)(2,1)} %param.3) | copy-start | bytes 1572868
  12.1 13.2 %copy-start.1 = (s32[32,16]{0,1:T(8,128)S(1)}, s32[32,16]{0,1:T(8,128)}, u32[]{:S(2)}) copy-start(s32[32,16]{0,1:T(8,128)} %param.4) | copy-start | bytes 6148
  12.1 125.4 %all-to-all-start = ((bf16[16,2048,128]{1,2,0:T(8,128)(2,1)}), bf16[16,2048,128]{1,2,0:T(8,128)(2,1)}, u32[]{:S(2)}, u32[]{:S(2)}) async-start(bf16[16,2048,128]{1,2,0:T(8,128)(2,1)} %stack.2), calls=%async_computation | async-start | bytes 16777216 | tf_op jit(solution)/shard_map/all_to_all | solution.py:12
  22.6 239.7 %reduce-scatter.4.cloned.1.call-start = ((), (), s32[]{:S(2)}) async-start(), calls=%async_computation.2 | async-start | bytes 1081344 | tf_op jit(solution)/shard_map/reduce_scatter | solution.py:49
  22.7 2.8 %collective-permute-start = (bf16[128,128]{1,0:T(8,128)(2,1)S(1)}, bf16[128,128]{1,0:T(8,128)(2,1)S(1)}, u32[]{:S(2)}, u32[]{:S(2)}) collective-permute-start(bf16[128,128]{1,0:T(8,128)(2,1)S(1)} %get-tuple-element.5), channel_id=1, source_target_pairs={{0,16},{16,32},{32,48},{48,64},{64,80},{80,96},{96,112},{112,128},... | collective-permute-start | bytes 98312 | tf_op jit(solution)/shard_map/ppermute | solution.py:20
  24.0 3.1 %collective-permute-start.1 = (bf16[128,128]{1,0:T(8,128)(2,1)S(1)}, bf16[128,128]{1,0:T(8,128)(2,1)S(1)}, u32[]{:S(2)}, u32[]{:S(2)}) collective-permute-start(bf16[128,128]{1,0:T(8,128)(2,1)S(1)} %get-tuple-element.6), channel_id=1, source_target_pairs={{16,0},{32,16},{48,32},{64,48},{80,64},{96,80},{112,96},{128,112},... | collective-permute-start | bytes 98312 | tf_op jit(solution)/shard_map/ppermute | solution.py:23
Sparse Core Ops, SparseCore 0:
  145.2 117.0 reduce-scatter.3
